TPU v7x, 128 devices: a whole 4x4x4 slice. The times are simulated.
128 devices in a mesh: row: 8 (over x, core), col: 16 (over z, y).
Axes of the slice: x: 4, y: 4, z: 4, core: 2. Of those that a mesh axis runs over, the one named last changes fastest.
Arguments:
- positions: float32 [3, 8, 1024, 256], P(None, 'row', 'col'), may hold values from -2 to 2
- strengths: float32 [3, 8, 1024, 256], P(None, 'row', 'col'), may hold values from -2 to 2
- live_count: int32 [8, 1024], P('row', 'col'), may hold values from 64 to 256, as said below
- send_list: int32 [8, 16, 16, 16], P('row', 'col'), may hold values from 0 to 63
- partner: int32 [8, 16, 16, 16], P('row', 'col'), may hold values from -1 to 63, as said below
- parent_block: int32 [8, 1024], P('row', 'col'), may hold values from 0 to 255
- parent_cell: int32 [8, 256], P('row'), may hold values from 0 to 63
Outputs:
- force: float32 [3, 8, 1024, 256], P(None, 'row', 'col')
- moments_cell: float32 [12, 8, 256], P(None, 'row', 'col')
- moments_top: float32 [12, 64], replicated
Inputs may be any that keep to these rules, and one draw needn't show every extreme that they name: `live_count`: segments at or past a block's live count are padding; some blocks in every draw are full. `partner`: -1 marks an empty slot; for each sender and receiver the used slots come first, and some sender fills all 16 slots to some receiver.
All inputs are finite; a program needn't handle non-finite values.
Results may differ from a plain program's by a relative error of at most 0.00013.
Values sent between devices are 32-bit elements; how exact they have to be, the bound alone decides.
A program may use at most 64 MiB of HBM per device.

v0:
```python
import math

import jax
import jax.numpy as jnp
from jax import lax
from jax.sharding import PartitionSpec as P

C2 = 64


CORE_SQUARED = 1.0
MOMENT_UNIT = 0.0625
PRECISE = lax.Precision.HIGHEST


def pair_weight(pos_row, str_row, pos_col, str_col):
    squared = CORE_SQUARED
    coupling = 0.0
    for component in range(3):
        offset = pos_row[:, component, :, None] - pos_col[:, component, None, :]
        squared = squared + offset * offset
        coupling = coupling + str_row[:, component, :, None] * str_col[:, component, None, :]
    return coupling / (squared * jnp.sqrt(squared))


def row_force(weight, pos_row, pos_col):
    return pos_row * jnp.sum(weight, axis=2)[:, None, :] - jnp.einsum(
        "pij,pcj->pci", weight, pos_col, precision=PRECISE
    )


def col_force(weight, pos_row, pos_col):
    return pos_col * jnp.sum(weight, axis=1)[:, None, :] - jnp.einsum(
        "pij,pci->pcj", weight, pos_row, precision=PRECISE
    )


def over_pairs(pos_row, str_row, pos_col, str_col):
    total = pos_row.shape[0]
    group = math.gcd(total, 16)

    def shaped(array):
        return array.reshape((total // group, group) + array.shape[1:])

    def per_group(group_items):
        group_pos_row, group_str_row, group_pos_col, group_str_col = group_items
        weight = pair_weight(group_pos_row, group_str_row, group_pos_col, group_str_col)
        outputs = []
        outputs.append(row_force(weight, group_pos_row, group_pos_col))
        outputs.append(col_force(weight, group_pos_row, group_pos_col))
        return tuple(outputs)

    results = lax.map(
        per_group, (shaped(pos_row), shaped(str_row), shaped(pos_col), shaped(str_col))
    )
    return [result.reshape((total,) + result.shape[2:]) for result in results]


def block_moments(pos_blocks, str_blocks):
    monopole = jnp.sum(str_blocks, axis=-1)
    dipole = jnp.einsum("bcs,bls->bcl", str_blocks, pos_blocks, precision=PRECISE)
    dipole = dipole.reshape(dipole.shape[0], 9)
    return jnp.concatenate([monopole, dipole], axis=-1) * MOMENT_UNIT


def body(positions, strengths, live_count, send_list, partner, parent_block, parent_cell):
    width = lax.axis_size("col")
    blocks = positions.shape[2]
    seg_len = positions.shape[3]
    slot_len = send_list.shape[3]
    pairs = width * slot_len
    seg_ids = jnp.arange(seg_len, dtype=jnp.int32)
    live_mask = (seg_ids[None, :] < live_count[0][:, None]).astype(jnp.float32)
    own_pos = jnp.transpose(positions[:, 0], (1, 0, 2))
    own_str = jnp.transpose(strengths[:, 0], (1, 0, 2)) * live_mask[:, None, :]
    targets = send_list[0, 0]
    slab_pos, slab_str = (
        lax.all_gather(own_pos, "col", axis=0, tiled=True),
        lax.all_gather(own_str, "col", axis=0, tiled=True),
    )
    slab_lists = lax.all_gather(send_list[0], "col", axis=0, tiled=True)
    mine = lax.dynamic_index_in_dim(slab_lists, lax.axis_index("col"), 1, keepdims=False)
    chosen = mine + jnp.arange(width, dtype=jnp.int32)[:, None] * blocks
    recv_pos = slab_pos[chosen]
    recv_str = slab_str[chosen]
    sources = partner[0, 0]
    is_valid = (sources >= 0).astype(jnp.float32)
    picked = jnp.maximum(sources, 0)
    near_pos = own_pos[picked]
    near_str = own_str[picked] * is_valid[:, :, None, None]

    def flatten(array):
        return array.reshape((pairs,) + array.shape[2:])

    force_recv, force_near = over_pairs(
        flatten(recv_pos), flatten(recv_str), flatten(near_pos), flatten(near_str)
    )
    returned = lax.all_to_all(
        force_recv.reshape(width, slot_len, 3, seg_len),
        "col",
        split_axis=0,
        concat_axis=0,
        tiled=True,
    )
    block_ids = jnp.arange(blocks, dtype=jnp.int32)
    near_hot = (picked.reshape(pairs)[:, None] == block_ids[None, :]).astype(
        jnp.float32
    ) * is_valid.reshape(pairs)[:, None]
    sent_hot = (targets.reshape(pairs)[:, None] == block_ids[None, :]).astype(jnp.float32)
    total = jnp.einsum("pb,pcs->bcs", near_hot, force_near, precision=PRECISE)
    total = total + jnp.einsum(
        "pb,pcs->bcs", sent_hot, returned.reshape(pairs, 3, seg_len), precision=PRECISE
    )
    force = jnp.transpose(total, (1, 0, 2))[:, None]
    moments = block_moments(own_pos, own_str)
    slab_cells = parent_cell.shape[1]
    share = slab_cells // width
    cell_hot = (
        parent_block[0][:, None] == jnp.arange(slab_cells, dtype=jnp.int32)[None, :]
    ).astype(jnp.float32)
    partial_sums = jnp.einsum("bm,bc->mc", moments, cell_hot, precision=PRECISE)
    cell_sums = lax.psum_scatter(partial_sums, "col", scatter_dimension=1, tiled=True)
    top_ids = jnp.arange(C2, dtype=jnp.int32)
    own_cells = lax.dynamic_slice_in_dim(parent_cell[0], lax.axis_index("col") * share, share)
    top_hot = (own_cells[:, None] == top_ids[None, :]).astype(jnp.float32)
    top_part = jnp.dot(cell_sums, top_hot, precision=PRECISE, preferred_element_type=jnp.float32)
    moments_top = lax.psum(top_part, ("row", "col"))
    return (force, cell_sums[:, None, :], moments_top)


def solution(mesh):
    placed = (
        P(None, "row", "col", None),
        P(None, "row", "col", None),
        P("row", "col"),
        P("row", "col", None, None),
        P("row", "col", None, None),
        P("row", "col"),
        P("row", None),
    )
    return jax.shard_map(
        body,
        mesh=mesh,
        in_specs=placed,
        out_specs=(P(None, "row", "col", None), P(None, "row", "col"), P()),
        check_vma=False,
    )
```

profile of v0, /device:TPU:0, one launch (start us, length us, event | category | flops | bytes accessed | tf_op | source)
XLA Modules:
  0.0 628.3 jit_solution(9759943110862105248)
XLA Ops:
  16.1 25.3 %all-gather = s32[16,1,16,16]{3,2,1,0:T(8,128)S(1)} all-gather(s32[1,1,16,16]{3,2,1,0:T(8,128)S(1)} %copy-done.4), channel_id=2, replica_groups=mesh['row'=8,'col'=16] {'col'}, dimensions={0}, use_global_device_ids=true | all-gather | bytes 17408 | tf_op jit(solution)/shard_map/all_gather | solution.py:81
  43.1 17.7 %all-gather.6.cloned.1.call-done = f32[1024,3,256]{2,0,1:T(8,128)} async-done(((f32[64,3,256]{2,0,1:T(8,128)}), f32[1024,3,256]{2,0,1:T(8,128)}) %all-gather.6.cloned.1.call-update) | async-done | bytes 3145744 | tf_op jit(solution)/shard_map/all_gather | solution.py:79
  70.4 40.0 %all-gather.4.cloned.1.call-done = f32[1024,3,256]{2,0,1:T(8,128)} async-done(((f32[64,3,256]{2,0,1:T(8,128)}), f32[1024,3,256]{2,0,1:T(8,128)}) %all-gather.4.cloned.1.call-update) | async-done | bytes 3145744 | tf_op jit(solution)/shard_map/all_gather | solution.py:78
  119.9 354.1 %while.12 = (s32[]{:T(128)}, f32[16,16,3,256]{3,1,2,0:T(8,128)}, f32[16,16,3,256]{3,2,1,0:T(4,128)}, f32[16,16,3,256]{3,2,1,0:T(4,128)S(1)}, f32[16,16,3,256]{3,...) while((s32[]{:T(128)}, f32[16,16,3,256]{3,1,2,0:T(8,128)}, ...), condition=%wide.region_3.4_spmd, body=%wide.region_0.3_spmd.sunk | while | flops 127967232 | bytes 2049121 | solution.py:53
  126.1 7.4 %fusion.61 = f32[16,16,3,256]{3,2,1,0:T(4,128)} fusion(f32[16,16,3,256]{3,2,1,0:T(4,128)} %get-tuple-element.186, s32[]{:T(128)} %get-tuple-element.184, f32[16,3,256]{2,1,0:T(4,128)S(1)} %get-tuple-element.162, f32[16,256]{1,0:T(8,128)S(1)} %bitcast.144, f32[16,256]{1,0:T(8,128)S(1)} %bitcast.147, f32[16,256]{1,0:T(8,128)S(1)} %bitcast.150, ...), kind=kOutput, calls=%fused_computation.8.clone.1 | convolution fusion | flops 54550528 | bytes 377344 | tf_op jit(solution)/shard_map/while/body/eval_jaxpr/pij,pci->pcj/dot_general | solution.py:33
  133.5 7.9 %fusion.60 = f32[1,16,3,256]{3,2,1,0:T(4,128)S(1)} fusion(f32[16,3,256]{2,1,0:T(4,128)S(1)} %get-tuple-element.160, f32[16,256]{1,0:T(8,128)S(1)} %bitcast.145, f32[16,256]{1,0:T(8,128)S(1)} %bitcast.148, f32[16,256]{1,0:T(8,128)S(1)} %bitcast.151, f32[16,256]{1,0:T(8,128)S(1)} %bitcast.154, f32[16,256]{1,0:T(8,128)S(1)} %bitcast.157, ...), kind=kOutput, calls=%fused_computation.10.clone.1 | convolution fusion | flops 54550528 | bytes 360448 | tf_op jit(solution)/shard_map/while/body/eval_jaxpr/pij,pcj->pci/dot_general | solution.py:27
  155.6 7.9 %fusion.60 = f32[1,16,3,256]{3,2,1,0:T(4,128)S(1)} fusion(f32[16,3,256]{2,1,0:T(4,128)S(1)} %get-tuple-element.160, f32[16,256]{1,0:T(8,128)S(1)} %bitcast.145, f32[16,256]{1,0:T(8,128)S(1)} %bitcast.148, f32[16,256]{1,0:T(8,128)S(1)} %bitcast.151, f32[16,256]{1,0:T(8,128)S(1)} %bitcast.154, f32[16,256]{1,0:T(8,128)S(1)} %bitcast.157, ...), kind=kOutput, calls=%fused_computation.10.clone.1 | convolution fusion | flops 54550528 | bytes 360448 | tf_op jit(solution)/shard_map/while/body/eval_jaxpr/pij,pcj->pci/dot_general | solution.py:27
  177.7 7.9 %fusion.60 = f32[1,16,3,256]{3,2,1,0:T(4,128)S(1)} fusion(f32[16,3,256]{2,1,0:T(4,128)S(1)} %get-tuple-element.160, f32[16,256]{1,0:T(8,128)S(1)} %bitcast.145, f32[16,256]{1,0:T(8,128)S(1)} %bitcast.148, f32[16,256]{1,0:T(8,128)S(1)} %bitcast.151, f32[16,256]{1,0:T(8,128)S(1)} %bitcast.154, f32[16,256]{1,0:T(8,128)S(1)} %bitcast.157, ...), kind=kOutput, calls=%fused_computation.10.clone.1 | convolution fusion | flops 54550528 | bytes 360448 | tf_op jit(solution)/shard_map/while/body/eval_jaxpr/pij,pcj->pci/dot_general | solution.py:27
  192.4 7.4 %fusion.61 = f32[16,16,3,256]{3,2,1,0:T(4,128)} fusion(f32[16,16,3,256]{3,2,1,0:T(4,128)} %get-tuple-element.186, s32[]{:T(128)} %get-tuple-element.184, f32[16,3,256]{2,1,0:T(4,128)S(1)} %get-tuple-element.162, f32[16,256]{1,0:T(8,128)S(1)} %bitcast.144, f32[16,256]{1,0:T(8,128)S(1)} %bitcast.147, f32[16,256]{1,0:T(8,128)S(1)} %bitcast.150, ...), kind=kOutput, calls=%fused_computation.8.clone.1 | convolution fusion | flops 54550528 | bytes 377344 | tf_op jit(solution)/shard_map/while/body/eval_jaxpr/pij,pci->pcj/dot_general | solution.py:33
  199.9 7.9 %fusion.60 = f32[1,16,3,256]{3,2,1,0:T(4,128)S(1)} fusion(f32[16,3,256]{2,1,0:T(4,128)S(1)} %get-tuple-element.160, f32[16,256]{1,0:T(8,128)S(1)} %bitcast.145, f32[16,256]{1,0:T(8,128)S(1)} %bitcast.148, f32[16,256]{1,0:T(8,128)S(1)} %bitcast.151, f32[16,256]{1,0:T(8,128)S(1)} %bitcast.154, f32[16,256]{1,0:T(8,128)S(1)} %bitcast.157, ...), kind=kOutput, calls=%fused_computation.10.clone.1 | convolution fusion | flops 54550528 | bytes 360448 | tf_op jit(solution)/shard_map/while/body/eval_jaxpr/pij,pcj->pci/dot_general | solution.py:27
  222.0 7.9 %fusion.60 = f32[1,16,3,256]{3,2,1,0:T(4,128)S(1)} fusion(f32[16,3,256]{2,1,0:T(4,128)S(1)} %get-tuple-element.160, f32[16,256]{1,0:T(8,128)S(1)} %bitcast.145, f32[16,256]{1,0:T(8,128)S(1)} %bitcast.148, f32[16,256]{1,0:T(8,128)S(1)} %bitcast.151, f32[16,256]{1,0:T(8,128)S(1)} %bitcast.154, f32[16,256]{1,0:T(8,128)S(1)} %bitcast.157, ...), kind=kOutput, calls=%fused_computation.10.clone.1 | convolution fusion | flops 54550528 | bytes 360448 | tf_op jit(solution)/shard_map/while/body/eval_jaxpr/pij,pcj->pci/dot_general | solution.py:27
  236.7 7.4 %fusion.61 = f32[16,16,3,256]{3,2,1,0:T(4,128)} fusion(f32[16,16,3,256]{3,2,1,0:T(4,128)} %get-tuple-element.186, s32[]{:T(128)} %get-tuple-element.184, f32[16,3,256]{2,1,0:T(4,128)S(1)} %get-tuple-element.162, f32[16,256]{1,0:T(8,128)S(1)} %bitcast.144, f32[16,256]{1,0:T(8,128)S(1)} %bitcast.147, f32[16,256]{1,0:T(8,128)S(1)} %bitcast.150, ...), kind=kOutput, calls=%fused_computation.8.clone.1 | convolution fusion | flops 54550528 | bytes 377344 | tf_op jit(solution)/shard_map/while/body/eval_jaxpr/pij,pci->pcj/dot_general | solution.py:33
  244.1 7.9 %fusion.60 = f32[1,16,3,256]{3,2,1,0:T(4,128)S(1)} fusion(f32[16,3,256]{2,1,0:T(4,128)S(1)} %get-tuple-element.160, f32[16,256]{1,0:T(8,128)S(1)} %bitcast.145, f32[16,256]{1,0:T(8,128)S(1)} %bitcast.148, f32[16,256]{1,0:T(8,128)S(1)} %bitcast.151, f32[16,256]{1,0:T(8,128)S(1)} %bitcast.154, f32[16,256]{1,0:T(8,128)S(1)} %bitcast.157, ...), kind=kOutput, calls=%fused_computation.10.clone.1 | convolution fusion | flops 54550528 | bytes 360448 | tf_op jit(solution)/shard_map/while/body/eval_jaxpr/pij,pcj->pci/dot_general | solution.py:27
  258.8 7.4 %fusion.61 = f32[16,16,3,256]{3,2,1,0:T(4,128)} fusion(f32[16,16,3,256]{3,2,1,0:T(4,128)} %get-tuple-element.186, s32[]{:T(128)} %get-tuple-element.184, f32[16,3,256]{2,1,0:T(4,128)S(1)} %get-tuple-element.162, f32[16,256]{1,0:T(8,128)S(1)} %bitcast.144, f32[16,256]{1,0:T(8,128)S(1)} %bitcast.147, f32[16,256]{1,0:T(8,128)S(1)} %bitcast.150, ...), kind=kOutput, calls=%fused_computation.8.clone.1 | convolution fusion | flops 54550528 | bytes 377344 | tf_op jit(solution)/shard_map/while/body/eval_jaxpr/pij,pci->pcj/dot_general | solution.py:33
  266.2 7.9 %fusion.60 = f32[1,16,3,256]{3,2,1,0:T(4,128)S(1)} fusion(f32[16,3,256]{2,1,0:T(4,128)S(1)} %get-tuple-element.160, f32[16,256]{1,0:T(8,128)S(1)} %bitcast.145, f32[16,256]{1,0:T(8,128)S(1)} %bitcast.148, f32[16,256]{1,0:T(8,128)S(1)} %bitcast.151, f32[16,256]{1,0:T(8,128)S(1)} %bitcast.154, f32[16,256]{1,0:T(8,128)S(1)} %bitcast.157, ...), kind=kOutput, calls=%fused_computation.10.clone.1 | convolution fusion | flops 54550528 | bytes 360448 | tf_op jit(solution)/shard_map/while/body/eval_jaxpr/pij,pcj->pci/dot_general | solution.py:27
  280.9 7.4 %fusion.61 = f32[16,16,3,256]{3,2,1,0:T(4,128)} fusion(f32[16,16,3,256]{3,2,1,0:T(4,128)} %get-tuple-element.186, s32[]{:T(128)} %get-tuple-element.184, f32[16,3,256]{2,1,0:T(4,128)S(1)} %get-tuple-element.162, f32[16,256]{1,0:T(8,128)S(1)} %bitcast.144, f32[16,256]{1,0:T(8,128)S(1)} %bitcast.147, f32[16,256]{1,0:T(8,128)S(1)} %bitcast.150, ...), kind=kOutput, calls=%fused_computation.8.clone.1 | convolution fusion | flops 54550528 | bytes 377344 | tf_op jit(solution)/shard_map/while/body/eval_jaxpr/pij,pci->pcj/dot_general | solution.py:33
  288.4 7.9 %fusion.60 = f32[1,16,3,256]{3,2,1,0:T(4,128)S(1)} fusion(f32[16,3,256]{2,1,0:T(4,128)S(1)} %get-tuple-element.160, f32[16,256]{1,0:T(8,128)S(1)} %bitcast.145, f32[16,256]{1,0:T(8,128)S(1)} %bitcast.148, f32[16,256]{1,0:T(8,128)S(1)} %bitcast.151, f32[16,256]{1,0:T(8,128)S(1)} %bitcast.154, f32[16,256]{1,0:T(8,128)S(1)} %bitcast.157, ...), kind=kOutput, calls=%fused_computation.10.clone.1 | convolution fusion | flops 54550528 | bytes 360448 | tf_op jit(solution)/shard_map/while/body/eval_jaxpr/pij,pcj->pci/dot_general | solution.py:27
  303.1 7.4 %fusion.61 = f32[16,16,3,256]{3,2,1,0:T(4,128)} fusion(f32[16,16,3,256]{3,2,1,0:T(4,128)} %get-tuple-element.186, s32[]{:T(128)} %get-tuple-element.184, f32[16,3,256]{2,1,0:T(4,128)S(1)} %get-tuple-element.162, f32[16,256]{1,0:T(8,128)S(1)} %bitcast.144, f32[16,256]{1,0:T(8,128)S(1)} %bitcast.147, f32[16,256]{1,0:T(8,128)S(1)} %bitcast.150, ...), kind=kOutput, calls=%fused_computation.8.clone.1 | convolution fusion | flops 54550528 | bytes 377344 | tf_op jit(solution)/shard_map/while/body/eval_jaxpr/pij,pci->pcj/dot_general | solution.py:33
  310.5 7.9 %fusion.60 = f32[1,16,3,256]{3,2,1,0:T(4,128)S(1)} fusion(f32[16,3,256]{2,1,0:T(4,128)S(1)} %get-tuple-element.160, f32[16,256]{1,0:T(8,128)S(1)} %bitcast.145, f32[16,256]{1,0:T(8,128)S(1)} %bitcast.148, f32[16,256]{1,0:T(8,128)S(1)} %bitcast.151, f32[16,256]{1,0:T(8,128)S(1)} %bitcast.154, f32[16,256]{1,0:T(8,128)S(1)} %bitcast.157, ...), kind=kOutput, calls=%fused_computation.10.clone.1 | convolution fusion | flops 54550528 | bytes 360448 | tf_op jit(solution)/shard_map/while/body/eval_jaxpr/pij,pcj->pci/dot_general | solution.py:27
  325.2 7.4 %fusion.61 = f32[16,16,3,256]{3,2,1,0:T(4,128)} fusion(f32[16,16,3,256]{3,2,1,0:T(4,128)} %get-tuple-element.186, s32[]{:T(128)} %get-tuple-element.184, f32[16,3,256]{2,1,0:T(4,128)S(1)} %get-tuple-element.162, f32[16,256]{1,0:T(8,128)S(1)} %bitcast.144, f32[16,256]{1,0:T(8,128)S(1)} %bitcast.147, f32[16,256]{1,0:T(8,128)S(1)} %bitcast.150, ...), kind=kOutput, calls=%fused_computation.8.clone.1 | convolution fusion | flops 54550528 | bytes 377344 | tf_op jit(solution)/shard_map/while/body/eval_jaxpr/pij,pci->pcj/dot_general | solution.py:33
  332.6 7.9 %fusion.60 = f32[1,16,3,256]{3,2,1,0:T(4,128)S(1)} fusion(f32[16,3,256]{2,1,0:T(4,128)S(1)} %get-tuple-element.160, f32[16,256]{1,0:T(8,128)S(1)} %bitcast.145, f32[16,256]{1,0:T(8,128)S(1)} %bitcast.148, f32[16,256]{1,0:T(8,128)S(1)} %bitcast.151, f32[16,256]{1,0:T(8,128)S(1)} %bitcast.154, f32[16,256]{1,0:T(8,128)S(1)} %bitcast.157, ...), kind=kOutput, calls=%fused_computation.10.clone.1 | convolution fusion | flops 54550528 | bytes 360448 | tf_op jit(solution)/shard_map/while/body/eval_jaxpr/pij,pcj->pci/dot_general | solution.py:27
  354.8 7.9 %fusion.60 = f32[1,16,3,256]{3,2,1,0:T(4,128)S(1)} fusion(f32[16,3,256]{2,1,0:T(4,128)S(1)} %get-tuple-element.160, f32[16,256]{1,0:T(8,128)S(1)} %bitcast.145, f32[16,256]{1,0:T(8,128)S(1)} %bitcast.148, f32[16,256]{1,0:T(8,128)S(1)} %bitcast.151, f32[16,256]{1,0:T(8,128)S(1)} %bitcast.154, f32[16,256]{1,0:T(8,128)S(1)} %bitcast.157, ...), kind=kOutput, calls=%fused_computation.10.clone.1 | convolution fusion | flops 54550528 | bytes 360448 | tf_op jit(solution)/shard_map/while/body/eval_jaxpr/pij,pcj->pci/dot_general | solution.py:27
  376.9 7.9 %fusion.60 = f32[1,16,3,256]{3,2,1,0:T(4,128)S(1)} fusion(f32[16,3,256]{2,1,0:T(4,128)S(1)} %get-tuple-element.160, f32[16,256]{1,0:T(8,128)S(1)} %bitcast.145, f32[16,256]{1,0:T(8,128)S(1)} %bitcast.148, f32[16,256]{1,0:T(8,128)S(1)} %bitcast.151, f32[16,256]{1,0:T(8,128)S(1)} %bitcast.154, f32[16,256]{1,0:T(8,128)S(1)} %bitcast.157, ...), kind=kOutput, calls=%fused_computation.10.clone.1 | convolution fusion | flops 54550528 | bytes 360448 | tf_op jit(solution)/shard_map/while/body/eval_jaxpr/pij,pcj->pci/dot_general | solution.py:27
  391.6 7.4 %fusion.61 = f32[16,16,3,256]{3,2,1,0:T(4,128)} fusion(f32[16,16,3,256]{3,2,1,0:T(4,128)} %get-tuple-element.186, s32[]{:T(128)} %get-tuple-element.184, f32[16,3,256]{2,1,0:T(4,128)S(1)} %get-tuple-element.162, f32[16,256]{1,0:T(8,128)S(1)} %bitcast.144, f32[16,256]{1,0:T(8,128)S(1)} %bitcast.147, f32[16,256]{1,0:T(8,128)S(1)} %bitcast.150, ...), kind=kOutput, calls=%fused_computation.8.clone.1 | convolution fusion | flops 54550528 | bytes 377344 | tf_op jit(solution)/shard_map/while/body/eval_jaxpr/pij,pci->pcj/dot_general | solution.py:33
  399.0 7.9 %fusion.60 = f32[1,16,3,256]{3,2,1,0:T(4,128)S(1)} fusion(f32[16,3,256]{2,1,0:T(4,128)S(1)} %get-tuple-element.160, f32[16,256]{1,0:T(8,128)S(1)} %bitcast.145, f32[16,256]{1,0:T(8,128)S(1)} %bitcast.148, f32[16,256]{1,0:T(8,128)S(1)} %bitcast.151, f32[16,256]{1,0:T(8,128)S(1)} %bitcast.154, f32[16,256]{1,0:T(8,128)S(1)} %bitcast.157, ...), kind=kOutput, calls=%fused_computation.10.clone.1 | convolution fusion | flops 54550528 | bytes 360448 | tf_op jit(solution)/shard_map/while/body/eval_jaxpr/pij,pcj->pci/dot_general | solution.py:27
  413.7 7.4 %fusion.61 = f32[16,16,3,256]{3,2,1,0:T(4,128)} fusion(f32[16,16,3,256]{3,2,1,0:T(4,128)} %get-tuple-element.186, s32[]{:T(128)} %get-tuple-element.184, f32[16,3,256]{2,1,0:T(4,128)S(1)} %get-tuple-element.162, f32[16,256]{1,0:T(8,128)S(1)} %bitcast.144, f32[16,256]{1,0:T(8,128)S(1)} %bitcast.147, f32[16,256]{1,0:T(8,128)S(1)} %bitcast.150, ...), kind=kOutput, calls=%fused_computation.8.clone.1 | convolution fusion | flops 54550528 | bytes 377344 | tf_op jit(solution)/shard_map/while/body/eval_jaxpr/pij,pci->pcj/dot_general | solution.py:33
  421.1 7.9 %fusion.60 = f32[1,16,3,256]{3,2,1,0:T(4,128)S(1)} fusion(f32[16,3,256]{2,1,0:T(4,128)S(1)} %get-tuple-element.160, f32[16,256]{1,0:T(8,128)S(1)} %bitcast.145, f32[16,256]{1,0:T(8,128)S(1)} %bitcast.148, f32[16,256]{1,0:T(8,128)S(1)} %bitcast.151, f32[16,256]{1,0:T(8,128)S(1)} %bitcast.154, f32[16,256]{1,0:T(8,128)S(1)} %bitcast.157, ...), kind=kOutput, calls=%fused_computation.10.clone.1 | convolution fusion | flops 54550528 | bytes 360448 | tf_op jit(solution)/shard_map/while/body/eval_jaxpr/pij,pcj->pci/dot_general | solution.py:27
  435.8 7.4 %fusion.61 = f32[16,16,3,256]{3,2,1,0:T(4,128)} fusion(f32[16,16,3,256]{3,2,1,0:T(4,128)} %get-tuple-element.186, s32[]{:T(128)} %get-tuple-element.184, f32[16,3,256]{2,1,0:T(4,128)S(1)} %get-tuple-element.162, f32[16,256]{1,0:T(8,128)S(1)} %bitcast.144, f32[16,256]{1,0:T(8,128)S(1)} %bitcast.147, f32[16,256]{1,0:T(8,128)S(1)} %bitcast.150, ...), kind=kOutput, calls=%fused_computation.8.clone.1 | convolution fusion | flops 54550528 | bytes 377344 | tf_op jit(solution)/shard_map/while/body/eval_jaxpr/pij,pci->pcj/dot_general | solution.py:33
  443.3 7.9 %fusion.60 = f32[1,16,3,256]{3,2,1,0:T(4,128)S(1)} fusion(f32[16,3,256]{2,1,0:T(4,128)S(1)} %get-tuple-element.160, f32[16,256]{1,0:T(8,128)S(1)} %bitcast.145, f32[16,256]{1,0:T(8,128)S(1)} %bitcast.148, f32[16,256]{1,0:T(8,128)S(1)} %bitcast.151, f32[16,256]{1,0:T(8,128)S(1)} %bitcast.154, f32[16,256]{1,0:T(8,128)S(1)} %bitcast.157, ...), kind=kOutput, calls=%fused_computation.10.clone.1 | convolution fusion | flops 54550528 | bytes 360448 | tf_op jit(solution)/shard_map/while/body/eval_jaxpr/pij,pcj->pci/dot_general | solution.py:27
  465.4 7.9 %fusion.60 = f32[1,16,3,256]{3,2,1,0:T(4,128)S(1)} fusion(f32[16,3,256]{2,1,0:T(4,128)S(1)} %get-tuple-element.160, f32[16,256]{1,0:T(8,128)S(1)} %bitcast.145, f32[16,256]{1,0:T(8,128)S(1)} %bitcast.148, f32[16,256]{1,0:T(8,128)S(1)} %bitcast.151, f32[16,256]{1,0:T(8,128)S(1)} %bitcast.154, f32[16,256]{1,0:T(8,128)S(1)} %bitcast.157, ...), kind=kOutput, calls=%fused_computation.10.clone.1 | convolution fusion | flops 54550528 | bytes 360448 | tf_op jit(solution)/shard_map/while/body/eval_jaxpr/pij,pcj->pci/dot_general | solution.py:27
  480.1 74.7 %all-reduce = f32[12,256]{1,0:T(8,128)S(1)} all-reduce(f32[12,256]{1,0:T(8,128)S(1)} %fusion.19), channel_id=3, replica_groups=mesh['row'=8,'col'=16] {'col'}, use_global_device_ids=true, to_apply=%region_5.6.clone | all-reduce | flops 3072 | bytes 24576
  555.8 62.6 %psum.7 = f32[12,64]{1,0:T(8,128)} all-reduce(f32[12,64]{1,0:T(8,128)S(1)} %fusion.27), channel_id=1, replica_groups=mesh['row'=8,'col'=16] {'row','col'}, use_global_device_ids=true, to_apply=%region_6.7 | all-reduce | flops 768 | bytes 6144 | tf_op jit(solution)/shard_map/psum | solution.py:127
  (291 shorter events, 190.3 us)
Async XLA Ops:
  7.2 548.3 %copy-start = (s32[1,256]{1,0:T(1,128)S(1)}, s32[1,256]{1,0:T(1,128)}, u32[]{:S(2)}) copy-start(s32[1,256]{1,0:T(1,128)} %param.15) | copy-start | bytes 3076
  7.2 8.9 %copy-start.4 = (s32[1,1,16,16]{3,2,1,0:T(8,128)S(1)}, s32[1,1,16,16]{3,2,1,0:T(8,128)}, u32[]{:S(2)}) copy-start(s32[1,1,16,16]{3,2,1,0:T(8,128)} %param.12) | copy-start | bytes 3076
  7.2 53.6 %all-gather.6.cloned.1.call-start = ((), (), s32[]{:S(2)}) async-start(), calls=%async_computation.2 | async-start | bytes 3342336 | tf_op jit(solution)/shard_map/all_gather | solution.py:79
  8.0 33.7 %copy-start.1 = (f32[3,1,64,256]{3,2,1,0:T(8,128)S(1)}, f32[3,1,64,256]{3,2,1,0:T(8,128)}, u32[]{:S(2)}) copy-start(f32[3,1,64,256]{3,2,1,0:T(8,128)} %param.10) | copy-start | bytes 589828
  8.0 33.7 %copy-start.2 = (f32[3,1,64,256]{3,2,1,0:T(8,128)S(1)}, f32[3,1,64,256]{3,2,1,0:T(8,128)}, u32[]{:S(2)}) copy-start(f32[3,1,64,256]{3,2,1,0:T(8,128)} %param.9) | copy-start | bytes 589828
  9.9 33.0 %copy-start.3 = (s32[1,1,16,16]{3,2,1,0:T(8,128)S(1)}, s32[1,1,16,16]{3,2,1,0:T(8,128)}, u32[]{:S(2)}) copy-start(s32[1,1,16,16]{3,2,1,0:T(8,128)} %param.13) | copy-start | bytes 3076
  10.0 100.5 %all-gather.4.cloned.1.call-start = ((), (), s32[]{:S(2)}) async-start(), calls=%async_computation.1 | async-start | bytes 3342336 | tf_op jit(solution)/shard_map/all_gather | solution.py:78
  119.9 358.6 %copy-start.5 = (s32[1,64]{1,0:T(1,128)S(1)}, s32[1,64]{1,0:T(1,128)}, u32[]{:S(2)}) copy-start(s32[1,64]{1,0:T(1,128)} %param.14) | copy-start | bytes 772
  119.9 358.9 %copy-start.6 = (u32[128]{0:T(128)S(1)}, u32[128]{0:T(128)}, u32[]{:S(2)}) copy-start(u32[128]{0:T(128)} %constant.55) | copy-start | bytes 1540
  474.0 146.3 %all-to-all-start = ((f32[16,16,3,256]{3,1,2,0:T(8,128)}), f32[16,16,3,256]{3,1,2,0:T(8,128)S(1)}, u32[]{:S(2)}, u32[]{:S(2)}) async-start(f32[16,16,3,256]{3,1,2,0:T(8,128)} %get-tuple-element.42), calls=%async_computation | async-start | bytes 1572864 | tf_op jit(solution)/shard_map/all_to_all | solution.py:98
Sparse Core Ops, SparseCore 0:
  10.2 50.5 all-gather.5
  63.5 46.8 all-gather.3
where the time goes:
time: 630 us; the launch traced here: 628 us
  matrix products  250 us (40%)
  blocking collectives  163 us (26%)
  other arithmetic  83.6 us (13%)
  waiting for transfers between devices  57.8 us (9%)
  local copies, waits for them, and re-layouts  53.2 us (8%)
  between operations  14.9 us (2%)
    dot_general x16, matrix products, row_force(): jnp.einsum('pij,pcj->pci', weight, pos_col, precision=PRECISE)  127 us
    dot_general x16, matrix products, col_force(): jnp.einsum('pij,pci->pcj', weight, pos_row, precision=PRECISE)  119 us
    reduce_sum x16, other arithmetic, col_force(): jnp.sum(weight, axis=1)[:, None, :]  80.5 us
    unnamed x1, blocking collectives  74.7 us
    psum x1, blocking collectives, body(): moments_top = lax.psum(top_part, ('row', 'col'))  62.6 us
    all_gather x1, waiting for transfers between devices, body(): lax.all_gather(own_pos, 'col', axis=0, tiled=True)  40 us
    all_gather x1, blocking collectives, body(): slab_lists = lax.all_gather(send_list[0], 'col', axis=0, tiled=True)  25.3 us
    all_gather x1, waiting for transfers between devices, body(): lax.all_gather(own_str, 'col', axis=0, tiled=True)  17.7 us
  transfers between devices with their start and end apart: 3, of which 2 were waited for; matrix products, arithmetic and copies ran while one was open for 3% of the time, Pallas kernels for 0%

commit v1 on v0

v1 whole, which is shorter than its diff:
```python
import functools

import jax
import jax.numpy as jnp
from jax import lax
from jax.experimental import pallas as pl
from jax.experimental.pallas import tpu as pltpu
from jax.sharding import PartitionSpec as P

C2 = 64
CORE_SQUARED = 1.0
MOMENT_UNIT = 0.0625
GROUP = 4
f32, bf16, i32 = jnp.float32, jnp.bfloat16, jnp.int32
MESH = pl.DeviceIdType.MESH


def split3(values):
    high = values.astype(bf16).astype(f32)
    rest = values - high
    middle = rest.astype(bf16).astype(f32)
    return high, middle, rest - middle


def dot(left, right, contract):
    return lax.dot_general(left, right, ((contract[0:1], contract[1:2]), ((), ())), preferred_element_type=f32)


def hot_dot(hot, values, contract=(1, 0)):
    high, middle, low = split3(values)
    return (
        dot(hot, high.astype(bf16), contract)
        + dot(hot, middle.astype(bf16), contract)
        + dot(hot, low.astype(bf16), contract)
    )


def row_ids(shape):
    return lax.broadcasted_iota(i32, shape, 0)


def tile_of(block):
    squares = block[0:1] * block[0:1] + block[1:2] * block[1:2] + block[2:3] * block[2:3]
    return jnp.concatenate([block[0:6], squares, jnp.ones_like(squares)], axis=0)


def distance_features(tile):
    high, middle, low = split3(tile)
    return jnp.concatenate([high, high, high, middle, middle, low], axis=0).astype(bf16)


def distance_coefficients(tile):
    row = row_ids(tile.shape)
    squares = tile[6:7] + CORE_SQUARED
    base = jnp.where(row < 3, -2.0 * tile, jnp.where(row == 7, squares, 0.0))
    high, middle, low = split3(base)
    unit = jnp.where(row == 6, 1.0, 0.0)
    first = jnp.where(row < 3, high, unit)
    second = jnp.where(row < 3, middle, 0.0)
    return jnp.concatenate([high + unit, middle, low, first, second, first], axis=0)


def strength_rows(block):
    width = block.shape[1]
    fours = [jnp.broadcast_to(block[c : c + 1], (4, width)) for c in (3, 4, 5)]
    return jnp.concatenate(fours + [jnp.zeros((4, width), f32)], axis=0)


def charge_features(block):
    one = jnp.ones((1, block.shape[1]), f32)
    four = [one, block[0:3]]
    rows = jnp.concatenate(four * 4, axis=0) * strength_rows(block)
    high = rows.astype(bf16).astype(f32)
    return jnp.concatenate([high, rows - high], axis=0).astype(bf16)


def force_rows(block, sums):
    products = sums * strength_rows(block)
    half = products[0:8] + products[8:16]
    summed = half[0:4] + half[4:8]
    return block[0:3] * summed[0:1] - summed[1:4]


def kernel(
    n_row, n_col, slots,
    send_smem, partner_smem, pos, strength, live, send_vmem, partner_vmem, parent_block, parent_cell,
    force, cell_out, top_out,
    turned, own, coef, charge, sent, received, back, returned, near, highs, lows,
    cell_sent, cell_got, top_sent, top_got, row_sent, row_got,
    sent_sem, received_sem, back_sem, returned_sem, cell_sent_sem, cell_got_sem, top_sent_sem, top_got_sem,
    row_sent_sem, row_got_sem,
):
    blocks, width = pos.shape[1], pos.shape[2]
    share = cell_got.shape[1]
    groups = slots // GROUP
    my_row, me = lax.axis_index("row"), lax.axis_index("col")

    barrier = pltpu.get_barrier_semaphore()

    def greet_col(step, carry):
        pl.semaphore_signal(barrier, inc=1, device_id={"col": lax.rem(me + step, n_col)}, device_id_type=MESH)
        return carry

    def greet_row(step, carry):
        pl.semaphore_signal(barrier, inc=1, device_id={"row": lax.rem(my_row + step, n_row)}, device_id_type=MESH)
        return carry

    lax.fori_loop(1, n_col, greet_col, 0)
    lax.fori_loop(1, n_row, greet_row, 0)

    same = row_ids((blocks, blocks)) == lax.broadcasted_iota(i32, (blocks, blocks), 1)
    counts = jnp.sum(jnp.where(same, live[...], 0).astype(f32), axis=1, keepdims=True)
    lane = lax.broadcasted_iota(i32, (blocks, width), 1).astype(f32)
    mask = jnp.where(lane < counts, 1.0, 0.0)
    x = [pos[c] for c in range(3)]
    q = [strength[c] * mask for c in range(3)]
    squares = x[0] * x[0] + x[1] * x[1] + x[2] * x[2]
    for c, rows in enumerate(x + q + [squares, jnp.ones_like(squares)]):
        for part in range(width // 128):
            turned[part, pl.ds(c, blocks, stride=8), :] = rows[:, part * 128 : part * 128 + 128]
    for part in range(width // 128):
        own[:, :, part * 128 : part * 128 + 128] = turned[part].reshape(blocks, 8, 128)

    def own_block(index):
        return own[index]

    def gather_to(target, receiver):
        for k in range(slots):
            target[receiver, k] = own_block(send_smem[receiver, k])[0:6]

    gather_to(received, me)
    pl.semaphore_wait(barrier, n_col + n_row - 2)

    def send_copy(peer):
        return pltpu.make_async_remote_copy(
            src_ref=sent.at[peer], dst_ref=received.at[me], send_sem=sent_sem.at[peer],
            recv_sem=received_sem.at[me], device_id={"col": peer}, device_id_type=MESH)

    def arrival(peer):
        return pltpu.make_async_remote_copy(
            src_ref=sent.at[peer], dst_ref=received.at[peer], send_sem=sent_sem.at[peer],
            recv_sem=received_sem.at[peer], device_id={"col": peer}, device_id_type=MESH)

    def back_copy(peer):
        return pltpu.make_async_remote_copy(
            src_ref=back.at[peer], dst_ref=returned.at[me], send_sem=back_sem.at[peer],
            recv_sem=returned_sem.at[me], device_id={"col": peer}, device_id_type=MESH)

    def back_arrival(peer):
        return pltpu.make_async_remote_copy(
            src_ref=back.at[peer], dst_ref=returned.at[peer], send_sem=back_sem.at[peer],
            recv_sem=returned_sem.at[peer], device_id={"col": peer}, device_id_type=MESH)

    def cell_copy(peer, at):
        return pltpu.make_async_remote_copy(
            src_ref=cell_sent.at[peer], dst_ref=cell_got.at[at], send_sem=cell_sent_sem.at[peer],
            recv_sem=cell_got_sem.at[at], device_id={"col": peer}, device_id_type=MESH)

    def top_copy(peer, at):
        return pltpu.make_async_remote_copy(
            src_ref=top_sent, dst_ref=top_got.at[at], send_sem=top_sent_sem.at[peer],
            recv_sem=top_got_sem.at[at], device_id={"col": peer}, device_id_type=MESH)

    def row_copy(peer, at):
        return pltpu.make_async_remote_copy(
            src_ref=row_sent, dst_ref=row_got.at[at], send_sem=row_sent_sem.at[peer],
            recv_sem=row_got_sem.at[at], device_id={"row": peer}, device_id_type=MESH)

    def send_step(step, carry):
        peer = lax.rem(me + n_col - step, n_col)
        gather_to(sent, peer)
        send_copy(peer).start()
        return carry

    lax.fori_loop(1, n_col, send_step, 0)

    columns = lax.broadcasted_iota(i32, (blocks, 128), 1)
    moments = jnp.zeros((blocks, 128), f32)
    terms = q + [q[c] * x[l] for c in range(3) for l in range(3)]
    for m, term in enumerate(terms):
        moments = jnp.where(columns == m, jnp.sum(term, axis=1, keepdims=True), moments)
    moments = moments * MOMENT_UNIT
    cells = n_col * share
    cell_hot = jnp.where(row_ids((cells, blocks)) == parent_block[...], 1.0, 0.0).astype(bf16)
    cell_part = hot_dot(cell_hot, moments)
    cell_sent[...] = cell_part.reshape(n_col, share, 128)
    cell_got[me] = cell_sent[me]
    top_hot = jnp.where(row_ids((C2, cells)) == parent_cell[...], 1.0, 0.0).astype(bf16)
    top_part = hot_dot(top_hot, cell_part)
    padded = jnp.concatenate([top_part, jnp.zeros((128 - C2, 128), f32)], axis=0)
    top_sent[...] = jnp.transpose(padded)[0:16]
    top_got[me] = top_sent[...]

    def moment_step(step, carry):
        peer = lax.rem(me + n_col - step, n_col)
        cell_copy(peer, me).start()
        top_copy(peer, me).start()
        return carry

    lax.fori_loop(1, n_col, moment_step, 0)

    def prepare(block, carry):
        tile = own_block(block)
        coef[block] = jnp.transpose(distance_coefficients(tile)).astype(bf16)
        charge[block] = charge_features(tile)
        return carry

    lax.fori_loop(0, blocks, prepare, 0)

    def partner_of(sender, k):
        return jnp.maximum(partner_smem[sender, k], 0)

    def compute(sender, group, slot):
        for u in range(GROUP):
            k = group * GROUP + u
            features = distance_features(tile_of(received[sender, k]))
            squared = dot(coef[partner_of(sender, k)], features, (1, 0))
            inverse = lax.rsqrt(squared)
            cubed = inverse * inverse * inverse
            high = cubed.astype(bf16)
            highs[slot, u] = high
            lows[slot, u] = (cubed - high.astype(f32)).astype(bf16)

    def use(sender, group, slot):
        for u in range(GROUP):
            k = group * GROUP + u
            near_at = partner_of(sender, k)
            block = received[sender, k]
            high, low = highs[slot, u], lows[slot, u]
            own_charge = charge[near_at]
            sums = dot(own_charge, high, (1, 0))
            sums = sums[0:16] + sums[16:32] + dot(own_charge[0:16], low, (1, 0))
            valid = jnp.clip(partner_smem[sender, k] + 1, 0, 1).astype(f32)
            rows = force_rows(block, sums) * valid
            for l in range(3):
                back[sender, l, k : k + 1] = rows[l : l + 1]
            far_charge = charge_features(block)
            sums = dot(far_charge, high, (1, 1))
            sums = sums[0:16] + sums[16:32] + dot(far_charge[0:16], low, (1, 1))
            rows = force_rows(own_block(near_at), sums)
            for l in range(3):
                near[l, sender, k : k + 1] = rows[l : l + 1]

    def sum_of(got, count):
        total = got[0]
        for at in range(1, count):
            total = total + got[at]
        return total

    compute(me, 0, 0)

    def sender_step(step, carry):
        sender = lax.rem(me + step, n_col)
        following = lax.rem(me + step + 1, n_col)
        for group in range(groups - 1):
            compute(sender, group + 1, (group + 1) % 2)
            use(sender, group, group % 2)

        @pl.when(step < n_col - 1)
        def _():
            arrival(following).wait_recv()

        compute(following, 0, 0)
        use(sender, groups - 1, (groups - 1) % 2)

        @pl.when(step > 0)
        def _():
            back_copy(sender).start()

        @pl.when(step == 4)
        def _():
            def wait_moments(other, inner):
                peer = lax.rem(me + other, n_col)
                cell_copy(peer, peer).wait_recv()
                top_copy(peer, peer).wait_recv()
                return inner

            lax.fori_loop(1, n_col, wait_moments, 0)
            cell_sum = sum_of(cell_got, n_col)
            cell_rows = jnp.concatenate([cell_sum, jnp.zeros((128 - share, 128), f32)], axis=0)
            cell_out[...] = jnp.transpose(cell_rows)[0:12, 0:share]
            row_sent[...] = sum_of(top_got, n_col)
            row_got[my_row] = row_sent[...]

            def row_step(other, inner):
                row_copy(lax.rem(my_row + other, n_row), my_row).start()
                return inner

            lax.fori_loop(1, n_row, row_step, 0)

        return carry

    lax.fori_loop(0, n_col, sender_step, 0)

    returned[me] = back[me]

    def row_wait(other, carry):
        peer = lax.rem(my_row + other, n_row)
        row_copy(peer, peer).wait_recv()
        return carry

    lax.fori_loop(1, n_row, row_wait, 0)
    top_out[...] = sum_of(row_got, n_row)[0:12, 0:C2]

    pairs = n_col * slots
    pair = lax.broadcasted_iota(i32, (slots, pairs), 1)
    pair_row = row_ids((slots, pairs))
    in_slot = jnp.where(lax.rem(pair, slots) == pair_row, 1.0, 0.0).astype(bf16)
    pair_c = lax.broadcasted_iota(i32, (n_col, pairs), 1)
    in_peer = jnp.where(lax.div(pair_c, slots) == row_ids((n_col, pairs)), 1.0, 0.0)
    block_id = row_ids((blocks, pairs)).astype(f32)

    def hot_of(listed):
        spread = dot(listed[...].astype(f32).astype(bf16), in_slot, (1, 0))
        flat = jnp.sum(spread * in_peer, axis=0, keepdims=True)
        return jnp.where(block_id == flat, 1.0, 0.0).astype(bf16)

    near_hot = hot_of(partner_vmem)
    totals = [hot_dot(near_hot, near[l].reshape(pairs, width)) for l in range(3)]
    sent_hot = hot_of(send_vmem)

    def finish(step, carry):
        peer = lax.rem(me + step, n_col)
        back_arrival(peer).wait_recv()
        return carry

    lax.fori_loop(1, n_col, finish, 0)
    for l in range(3):
        force[l] = totals[l] + hot_dot(sent_hot, returned[:, l].reshape(pairs, width))

    def drain(step, carry):
        peer = lax.rem(me + step, n_col)
        send_copy(peer).wait_send()
        back_copy(peer).wait_send()
        cell_copy(peer, me).wait_send()
        top_copy(peer, me).wait_send()
        return carry

    lax.fori_loop(1, n_col, drain, 0)

    def drain_row(step, carry):
        row_copy(lax.rem(my_row + step, n_row), my_row).wait_send()
        return carry

    lax.fori_loop(1, n_row, drain_row, 0)


def body(positions, strengths, live_count, send_list, partner, parent_block, parent_cell):
    n_row, n_col = lax.axis_size("row"), lax.axis_size("col")
    blocks, width = positions.shape[2:]
    slots = send_list.shape[3]
    cells = parent_cell.shape[1]
    share = cells // n_col
    vmem = pl.BlockSpec(memory_space=pltpu.VMEM)
    smem = pl.BlockSpec(memory_space=pltpu.SMEM)
    dma = pltpu.SemaphoreType.DMA
    sends, partners = send_list[0, 0], partner[0, 0]
    force, cell, top = pl.pallas_call(
        functools.partial(kernel, n_row, n_col, slots),
        out_shape=(
            jax.ShapeDtypeStruct((3, blocks, width), f32),
            jax.ShapeDtypeStruct((12, share), f32),
            jax.ShapeDtypeStruct((12, C2), f32),
        ),
        in_specs=[smem, smem] + [vmem] * 7,
        out_specs=(vmem, vmem, vmem),
        scratch_shapes=[
            pltpu.VMEM((width // 128, blocks * 8, 128), f32),
            pltpu.VMEM((blocks, 8, width), f32),
            pltpu.VMEM((blocks, width, 48), bf16),
            pltpu.VMEM((blocks, 32, width), bf16),
            pltpu.VMEM((n_col, slots, 6, width), f32),
            pltpu.VMEM((n_col, slots, 6, width), f32),
            pltpu.VMEM((n_col, 3, slots, width), f32),
            pltpu.VMEM((n_col, 3, slots, width), f32),
            pltpu.VMEM((3, n_col, slots, width), f32),
            pltpu.VMEM((2, GROUP, width, width), bf16),
            pltpu.VMEM((2, GROUP, width, width), bf16),
            pltpu.VMEM((n_col, share, 128), f32),
            pltpu.VMEM((n_col, share, 128), f32),
            pltpu.VMEM((16, 128), f32),
            pltpu.VMEM((n_col, 16, 128), f32),
            pltpu.VMEM((16, 128), f32),
            pltpu.VMEM((n_row, 16, 128), f32),
            *[dma((n_col,)) for _ in range(8)],
            dma((n_row,)),
            dma((n_row,)),
        ],
        compiler_params=pltpu.CompilerParams(
            collective_id=0, has_side_effects=True, vmem_limit_bytes=40 * 1024 * 1024
        ),
        name="pair_forces",
    )(sends, partners, positions[:, 0], strengths[:, 0], live_count, sends, partners, parent_block, parent_cell)
    return force[:, None], cell[:, None, :], top


def solution(mesh):
    placed = (
        P(None, "row", "col", None),
        P(None, "row", "col", None),
        P("row", "col"),
        P("row", "col", None, None),
        P("row", "col", None, None),
        P("row", "col"),
        P("row", None),
    )
    return jax.shard_map(
        body,
        mesh=mesh,
        in_specs=placed,
        out_specs=(P(None, "row", "col", None), P(None, "row", "col"), P()),
        check_vma=False,
    )
```

time: 630 us -> 84.4 us (0.13)
  matrix products: 250 us -> 0 us
  blocking collectives: 163 us -> 0 us
  other arithmetic: 83.6 us -> 0 us
  Pallas kernels: 0 us -> 76.9 us
  waiting for transfers between devices: 57.8 us -> 0 us
  local copies, waits for them, and re-layouts: 53.2 us -> 5.79 us
  between operations: 14.9 us -> 0.67 us
    dot_general x37 -> x0, matrix products: 250 us -> none  [the longest x16 127 us: row_force(): jnp.einsum('pij,pcj->pci', weight, pos_col, precision=PRECISE)]
    reduce_sum x17 -> x0, other arithmetic: 80.8 us -> none  [the longest x16 80.5 us: col_force(): jnp.sum(weight, axis=1)[:, None, :]]
    pallas_call x0 -> x1, Pallas kernels: none -> 76.9 us  [body(): pl.pallas_call(functools.partial(kernel, n_row, n_col, slots), out_shape=...]
    unnamed x1 -> x0, blocking collectives: 74.7 us -> none
    psum x1 -> x0, blocking collectives: 62.6 us -> none  [body(): moments_top = lax.psum(top_part, ('row', 'col'))]
    all_gather x2 -> x0, waiting for transfers between devices: 57.7 us -> none  [the longest x1 40 us: body(): lax.all_gather(own_pos, 'col', axis=0, tiled=True)]
    all_gather x1 -> x0, blocking collectives: 25.3 us -> none  [body(): slab_lists = lax.all_gather(send_list[0], 'col', axis=0, tiled=True)]
    squeeze x48 -> x0, local copies, waits for them, and re-layouts: 14.2 us -> none  [over_pairs(): lax.map(per_group, (shaped(pos_row), shaped(str_row), shaped(pos_col), sh...]
  transfers between devices with their start and end apart: 3 -> 0, of which waited for: 2 -> 0; matrix products, arithmetic and copies ran while one was open for 3% -> 0% of each run, Pallas kernels for 0% -> 0%
where the time goes in v1:
time: 84.4 us; the launch traced here: 83.4 us
  Pallas kernels  76.9 us (91%)
  local copies, waits for them, and re-layouts  5.79 us (7%)
    pallas_call x1, Pallas kernels, body(): pl.pallas_call(functools.partial(kernel, n_row, n_col, slots), out_shape=...  76.9 us
    unnamed x17, local copies, waits for them, and re-layouts  5.79 us

profile of v1, /device:TPU:0, one launch (start us, length us, event | category | flops | bytes accessed | tf_op | source)
XLA Modules:
  0.0 83.4 jit_solution(16925088877631737121)
XLA Ops:
  0.6 0.0 copy-start.6
  0.6 0.0 copy-start.4
  0.7 0.0 copy-start.5
  0.7 0.6 copy-done.6
  1.3 0.0 copy-done.4
  1.3 0.0 copy-done.5
  1.3 0.0 copy-start
  1.3 0.9 %copy-done = f32[3,1,64,256]{3,2,1,0:T(8,128)S(1)} copy-done((f32[3,1,64,256]{3,2,1,0:T(8,128)S(1)}, f32[3,1,64,256]{3,2,1,0:T(8,128)}, u32[]{:S(2)}) %copy-start) | copy-done | bytes 196632
  2.3 0.0 copy-start.1
  2.3 0.9 %copy-done.1 = f32[3,1,64,256]{3,2,1,0:T(8,128)S(1)} copy-done((f32[3,1,64,256]{3,2,1,0:T(8,128)S(1)}, f32[3,1,64,256]{3,2,1,0:T(8,128)}, u32[]{:S(2)}) %copy-start.1) | copy-done | bytes 196632
  3.2 0.0 copy-start.2
  3.2 0.7 copy-done.2
  3.9 0.0 copy-start.3
  3.9 0.7 copy-done.3
  4.6 76.9 %pair_forces.1 = (f32[3,64,256]{2,1,0:T(8,128)S(1)}, f32[12,16]{1,0:T(8,128)S(1)}, f32[12,64]{1,0:T(8,128)S(1)}) custom-call(s32[16,16]{1,0:T(8,128)S(1)} %bitcast.11, s32[16,16]{1,0:T(8,128)S(1)} %bitcast.13, f32[3,64,256]{2,1,0:T(8,128)S(1)} %bitcast.9, f32[3,64,256]{2,1,0:T(8,128)S(1)} %bitcast.10, s32[1,64]{1,0:T(1,128)S(1)} %copy-done.5, ...), custom_call_target="tpu_custom_call" | custom-call | tf_op jit(solution)/shard_map/pair_forces/pallas_call | solution.py:358
  81.5 0.6 copy.11
  82.1 0.7 copy.14
  82.8 0.6 copy.15
Async XLA Ops:
  0.6 0.7 copy-start.6
  0.6 0.7 copy-start.4
  0.7 0.7 copy-start.5
  1.3 0.9 %copy-start = (f32[3,1,64,256]{3,2,1,0:T(8,128)S(1)}, f32[3,1,64,256]{3,2,1,0:T(8,128)}, u32[]{:S(2)}) copy-start(f32[3,1,64,256]{3,2,1,0:T(8,128)} %param.7) | copy-start | bytes 589828
  2.3 0.9 %copy-start.1 = (f32[3,1,64,256]{3,2,1,0:T(8,128)S(1)}, f32[3,1,64,256]{3,2,1,0:T(8,128)}, u32[]{:S(2)}) copy-start(f32[3,1,64,256]{3,2,1,0:T(8,128)} %param.8) | copy-start | bytes 589828
  3.2 0.7 copy-start.2
  3.9 0.7 copy-start.3

commit v2 on v1

--- a/solution.py
+++ b/solution.py
@@ -11,6 +11,17 @@
 CORE_SQUARED = 1.0
 MOMENT_UNIT = 0.0625
 GROUP = 4
+AHEAD = 6
+LINES = 6
+CHUNKS = 1
+PREPARED = 8
+RING = 4
+OFFSETS = (
+    (0, 1), (0, 3), (1, 0), (3, 0), (1, 1), (3, 3), (1, 3), (3, 1),
+    (0, 2), (2, 0), (2, 1), (2, 3), (1, 2), (3, 2), (2, 2),
+)
+CODE_Z = sum(offset[0] * RING**step for step, offset in enumerate(OFFSETS))
+CODE_Y = sum(offset[1] * RING**step for step, offset in enumerate(OFFSETS))
 f32, bf16, i32 = jnp.float32, jnp.bfloat16, jnp.int32
 MESH = pl.DeviceIdType.MESH
 
@@ -83,18 +94,37 @@
 
 def kernel(
     n_row, n_col, slots,
-    send_smem, partner_smem, pos, strength, live, send_vmem, partner_vmem, parent_block, parent_cell,
+    pos_in, strength_in, live_in, send_in, partner_in, parent_block_in, parent_cell_in,
     force, cell_out, top_out,
-    turned, own, coef, charge, sent, received, back, returned, near, highs, lows,
+    pos, strength, live, send_smem, partner_smem, send_vmem, partner_vmem, parent_block, parent_cell, turned, own, coef, charge, sent, received, back, returned, near, highs, lows,
     cell_sent, cell_got, top_sent, top_got, row_sent, row_got,
     sent_sem, received_sem, back_sem, returned_sem, cell_sent_sem, cell_got_sem, top_sent_sem, top_got_sem,
-    row_sent_sem, row_got_sem,
+    row_sent_sem, row_got_sem, input_sem,
 ):
+    moves = (
+        (live_in, live), (pos_in, pos), (strength_in, strength), (send_in, send_smem), (partner_in, partner_smem),
+        (send_in, send_vmem), (partner_in, partner_vmem), (parent_block_in, parent_block), (parent_cell_in, parent_cell),
+    )
+    inputs = [pltpu.make_async_copy(a, b, input_sem.at[at]) for at, (a, b) in enumerate(moves)]
+    for copy in inputs:
+        copy.start()
     blocks, width = pos.shape[1], pos.shape[2]
     share = cell_got.shape[1]
     groups = slots // GROUP
     my_row, me = lax.axis_index("row"), lax.axis_index("col")
 
+    my_z, my_y = lax.div(me, RING), lax.rem(me, RING)
+
+    def source(code):
+        return lax.rem(my_z + lax.rem(code[0], RING), RING) * RING + lax.rem(my_y + lax.rem(code[1], RING), RING)
+
+    def target(code):
+        z = lax.rem(my_z + RING - lax.rem(code[0], RING), RING)
+        return z * RING + lax.rem(my_y + RING - lax.rem(code[1], RING), RING)
+
+    def next_code(code):
+        return lax.div(code[0], RING), lax.div(code[1], RING)
+
     barrier = pltpu.get_barrier_semaphore()
 
     def greet_col(step, carry):
@@ -107,6 +137,9 @@
 
     lax.fori_loop(1, n_col, greet_col, 0)
     lax.fori_loop(1, n_row, greet_row, 0)
+
+    for copy in inputs:
+        copy.wait()
 
     same = row_ids((blocks, blocks)) == lax.broadcasted_iota(i32, (blocks, blocks), 1)
     counts = jnp.sum(jnp.where(same, live[...], 0).astype(f32), axis=1, keepdims=True)
@@ -124,9 +157,9 @@
     def own_block(index):
         return own[index]
 
-    def gather_to(target, receiver):
+    def gather_to(buffer, receiver):
         for k in range(slots):
-            target[receiver, k] = own_block(send_smem[receiver, k])[0:6]
+            buffer[receiver, LINES * k : LINES * k + LINES] = own_block(send_smem[receiver, k])[0:LINES]
 
     gather_to(received, me)
     pl.semaphore_wait(barrier, n_col + n_row - 2)
@@ -136,6 +169,14 @@
             src_ref=sent.at[peer], dst_ref=received.at[me], send_sem=sent_sem.at[peer],
             recv_sem=received_sem.at[me], device_id={"col": peer}, device_id_type=MESH)
 
+    def start_send(peer):
+        part = slots * LINES // CHUNKS
+        for chunk in range(CHUNKS):
+            lines = pl.ds(chunk * part, part)
+            pltpu.make_async_remote_copy(
+                src_ref=sent.at[peer, lines], dst_ref=received.at[me, lines], send_sem=sent_sem.at[peer],
+                recv_sem=received_sem.at[me], device_id={"col": peer}, device_id_type=MESH).start()
+
     def arrival(peer):
         return pltpu.make_async_remote_copy(
             src_ref=sent.at[peer], dst_ref=received.at[peer], send_sem=sent_sem.at[peer],
@@ -166,13 +207,24 @@
             src_ref=row_sent, dst_ref=row_got.at[at], send_sem=row_sent_sem.at[peer],
             recv_sem=row_got_sem.at[at], device_id={"row": peer}, device_id_type=MESH)
 
-    def send_step(step, carry):
-        peer = lax.rem(me + n_col - step, n_col)
+    def send_step(step, code):
+        peer = target(code)
         gather_to(sent, peer)
-        send_copy(peer).start()
-        return carry
-
-    lax.fori_loop(1, n_col, send_step, 0)
+        start_send(peer)
+        return next_code(code)
+
+    codes = (jnp.int32(CODE_Z), jnp.int32(CODE_Y))
+    send_code = lax.fori_loop(0, AHEAD, send_step, codes)
+
+    def prepare(step, carry):
+        for u in range(PREPARED):
+            block = step * PREPARED + u
+            tile = own_block(block)
+            coef[block] = jnp.transpose(distance_coefficients(tile)).astype(bf16)
+            charge[block] = charge_features(tile)
+        return carry
+
+    lax.fori_loop(0, blocks // PREPARED, prepare, 0)
 
     columns = lax.broadcasted_iota(i32, (blocks, 128), 1)
     moments = jnp.zeros((blocks, 128), f32)
@@ -199,21 +251,13 @@
 
     lax.fori_loop(1, n_col, moment_step, 0)
 
-    def prepare(block, carry):
-        tile = own_block(block)
-        coef[block] = jnp.transpose(distance_coefficients(tile)).astype(bf16)
-        charge[block] = charge_features(tile)
-        return carry
-
-    lax.fori_loop(0, blocks, prepare, 0)
-
     def partner_of(sender, k):
         return jnp.maximum(partner_smem[sender, k], 0)
 
     def compute(sender, group, slot):
         for u in range(GROUP):
             k = group * GROUP + u
-            features = distance_features(tile_of(received[sender, k]))
+            features = distance_features(tile_of(received[sender, LINES * k : LINES * k + LINES]))
             squared = dot(coef[partner_of(sender, k)], features, (1, 0))
             inverse = lax.rsqrt(squared)
             cubed = inverse * inverse * inverse
@@ -225,7 +269,7 @@
         for u in range(GROUP):
             k = group * GROUP + u
             near_at = partner_of(sender, k)
-            block = received[sender, k]
+            block = received[sender, LINES * k : LINES * k + LINES]
             high, low = highs[slot, u], lows[slot, u]
             own_charge = charge[near_at]
             sums = dot(own_charge, high, (1, 0))
@@ -247,23 +291,32 @@
             total = total + got[at]
         return total
 
-    compute(me, 0, 0)
+    first = source(codes)
+    arrival(first).wait_recv()
+    compute(first, 0, 0)
 
     def sender_step(step, carry):
-        sender = lax.rem(me + step, n_col)
-        following = lax.rem(me + step + 1, n_col)
+        code, send_code = carry[0:2], carry[2:4]
+        sender = source(code)
+        following_code = next_code(code)
+        following = source(following_code)
+
+        @pl.when(step + AHEAD < n_col - 1)
+        def _():
+            send_step(step, send_code)
+
         for group in range(groups - 1):
             compute(sender, group + 1, (group + 1) % 2)
             use(sender, group, group % 2)
 
-        @pl.when(step < n_col - 1)
+        @pl.when(step < n_col - 2)
         def _():
             arrival(following).wait_recv()
 
         compute(following, 0, 0)
         use(sender, groups - 1, (groups - 1) % 2)
 
-        @pl.when(step > 0)
+        @pl.when(step < n_col - 1)
         def _():
             back_copy(sender).start()
 
@@ -288,9 +341,9 @@
 
             lax.fori_loop(1, n_row, row_step, 0)
 
-        return carry
-
-    lax.fori_loop(0, n_col, sender_step, 0)
+        return following_code + next_code(send_code)
+
+    lax.fori_loop(0, n_col, sender_step, codes + send_code)
 
     returned[me] = back[me]
 
@@ -352,9 +405,8 @@
     cells = parent_cell.shape[1]
     share = cells // n_col
     vmem = pl.BlockSpec(memory_space=pltpu.VMEM)
-    smem = pl.BlockSpec(memory_space=pltpu.SMEM)
+    hbm = pl.BlockSpec(memory_space=pl.ANY)
     dma = pltpu.SemaphoreType.DMA
-    sends, partners = send_list[0, 0], partner[0, 0]
     force, cell, top = pl.pallas_call(
         functools.partial(kernel, n_row, n_col, slots),
         out_shape=(
@@ -362,15 +414,24 @@
             jax.ShapeDtypeStruct((12, share), f32),
             jax.ShapeDtypeStruct((12, C2), f32),
         ),
-        in_specs=[smem, smem] + [vmem] * 7,
+        in_specs=[hbm] * 7,
         out_specs=(vmem, vmem, vmem),
         scratch_shapes=[
+            pltpu.VMEM((3, blocks, width), f32),
+            pltpu.VMEM((3, blocks, width), f32),
+            pltpu.VMEM((1, blocks), i32),
+            pltpu.SMEM((n_col, slots), i32),
+            pltpu.SMEM((n_col, slots), i32),
+            pltpu.VMEM((n_col, slots), i32),
+            pltpu.VMEM((n_col, slots), i32),
+            pltpu.VMEM((1, blocks), i32),
+            pltpu.VMEM((1, cells), i32),
             pltpu.VMEM((width // 128, blocks * 8, 128), f32),
             pltpu.VMEM((blocks, 8, width), f32),
             pltpu.VMEM((blocks, width, 48), bf16),
             pltpu.VMEM((blocks, 32, width), bf16),
-            pltpu.VMEM((n_col, slots, 6, width), f32),
-            pltpu.VMEM((n_col, slots, 6, width), f32),
+            pltpu.VMEM((n_col, slots * LINES, width), f32),
+            pltpu.VMEM((n_col, slots * LINES, width), f32),
             pltpu.VMEM((n_col, 3, slots, width), f32),
             pltpu.VMEM((n_col, 3, slots, width), f32),
             pltpu.VMEM((3, n_col, slots, width), f32),
@@ -385,12 +446,13 @@
             *[dma((n_col,)) for _ in range(8)],
             dma((n_row,)),
             dma((n_row,)),
+            dma((9,)),
         ],
         compiler_params=pltpu.CompilerParams(
             collective_id=0, has_side_effects=True, vmem_limit_bytes=40 * 1024 * 1024
         ),
         name="pair_forces",
-    )(sends, partners, positions[:, 0], strengths[:, 0], live_count, sends, partners, parent_block, parent_cell)
+    )(positions[:, 0], strengths[:, 0], live_count, send_list[0, 0], partner[0, 0], parent_block, parent_cell)
     return force[:, None], cell[:, None, :], top
 
 

time: 84.4 us -> 66.5 us (0.79)
  Pallas kernels: 76.9 us -> 59.7 us
    pallas_call x1, Pallas kernels: 76.9 us -> 59.7 us  [body(): pl.pallas_call(functools.partial(kernel, n_row, n_col, slots), out_shape=...]
where the time goes in v2:
time: 66.5 us; the launch traced here: 66.2 us
  Pallas kernels  59.7 us (90%)
  local copies, waits for them, and re-layouts  5.79 us (9%)
  between operations  0.67 us (1%)
    pallas_call x1, Pallas kernels, body(): pl.pallas_call(functools.partial(kernel, n_row, n_col, slots), out_shape=...  59.7 us
    unnamed x17, local copies, waits for them, and re-layouts  5.79 us

profile of v2, /device:TPU:0, one launch (start us, length us, event | category | flops | bytes accessed | tf_op | source)
XLA Modules:
  0.0 66.2 jit_solution(11444699103942572999)
XLA Ops:
  0.6 0.0 copy-start.6
  0.6 0.0 copy-start.4
  0.7 0.0 copy-start.5
  0.7 0.6 copy-done.6
  1.3 0.0 copy-done.4
  1.3 0.0 copy-done.5
  1.3 0.0 copy-start
  1.3 0.9 %copy-done = f32[3,1,64,256]{3,2,1,0:T(8,128)S(1)} copy-done((f32[3,1,64,256]{3,2,1,0:T(8,128)S(1)}, f32[3,1,64,256]{3,2,1,0:T(8,128)}, u32[]{:S(2)}) %copy-start) | copy-done | bytes 196632
  2.3 0.0 copy-start.1
  2.3 0.9 %copy-done.1 = f32[3,1,64,256]{3,2,1,0:T(8,128)S(1)} copy-done((f32[3,1,64,256]{3,2,1,0:T(8,128)S(1)}, f32[3,1,64,256]{3,2,1,0:T(8,128)}, u32[]{:S(2)}) %copy-start.1) | copy-done | bytes 196632
  3.2 0.0 copy-start.2
  3.2 0.7 %copy-done.2 = s32[1,1,16,16]{3,2,1,0:T(8,128)S(1)} copy-done((s32[1,1,16,16]{3,2,1,0:T(8,128)S(1)}, s32[1,1,16,16]{3,2,1,0:T(8,128)}, u32[]{:S(2)}) %copy-start.2) | copy-done | bytes 1048
  3.9 0.0 copy-start.3
  3.9 0.7 %copy-done.3 = s32[1,1,16,16]{3,2,1,0:T(8,128)S(1)} copy-done((s32[1,1,16,16]{3,2,1,0:T(8,128)S(1)}, s32[1,1,16,16]{3,2,1,0:T(8,128)}, u32[]{:S(2)}) %copy-start.3) | copy-done | bytes 1048
  4.6 59.7 %pair_forces.1 = (f32[3,64,256]{2,1,0:T(8,128)S(1)}, f32[12,16]{1,0:T(8,128)S(1)}, f32[12,64]{1,0:T(8,128)S(1)}) custom-call(f32[3,64,256]{2,1,0:T(8,128)S(1)} %bitcast.8, f32[3,64,256]{2,1,0:T(8,128)S(1)} %bitcast.9, s32[1,64]{1,0:T(1,128)S(1)} %copy-done.5, s32[16,16]{1,0:T(8,128)S(1)} %bitcast.11, s32[16,16]{1,0:T(8,128)S(1)} %bitcast.12, ...), custom_call_target="tpu_custom_call" | custom-call | tf_op jit(solution)/shard_map/pair_forces/pallas_call | solution.py:410
  64.3 0.6 copy.11
  64.9 0.7 %copy.14 = f32[3,1,64,256]{3,2,1,0:T(8,128)} copy(f32[3,1,64,256]{3,2,1,0:T(8,128)S(1)} %bitcast.10) | data formatting | bytes 393216
  65.6 0.6 copy.15
Async XLA Ops:
  0.6 0.7 copy-start.6
  0.6 0.7 %copy-start.4 = (s32[1,256]{1,0:T(1,128)S(1)}, s32[1,256]{1,0:T(1,128)}, u32[]{:S(2)}) copy-start(s32[1,256]{1,0:T(1,128)} %parent_cell_in.1) | copy-start | bytes 3076
  0.7 0.7 %copy-start.5 = (s32[1,64]{1,0:T(1,128)S(1)}, s32[1,64]{1,0:T(1,128)}, u32[]{:S(2)}) copy-start(s32[1,64]{1,0:T(1,128)} %live_in.1) | copy-start | bytes 772
  1.3 0.9 %copy-start = (f32[3,1,64,256]{3,2,1,0:T(8,128)S(1)}, f32[3,1,64,256]{3,2,1,0:T(8,128)}, u32[]{:S(2)}) copy-start(f32[3,1,64,256]{3,2,1,0:T(8,128)} %param.7) | copy-start | bytes 589828
  2.3 0.9 %copy-start.1 = (f32[3,1,64,256]{3,2,1,0:T(8,128)S(1)}, f32[3,1,64,256]{3,2,1,0:T(8,128)}, u32[]{:S(2)}) copy-start(f32[3,1,64,256]{3,2,1,0:T(8,128)} %param.8) | copy-start | bytes 589828
  3.2 0.7 %copy-start.2 = (s32[1,1,16,16]{3,2,1,0:T(8,128)S(1)}, s32[1,1,16,16]{3,2,1,0:T(8,128)}, u32[]{:S(2)}) copy-start(s32[1,1,16,16]{3,2,1,0:T(8,128)} %param.10) | copy-start | bytes 3076
  3.9 0.7 %copy-start.3 = (s32[1,1,16,16]{3,2,1,0:T(8,128)S(1)}, s32[1,1,16,16]{3,2,1,0:T(8,128)}, u32[]{:S(2)}) copy-start(s32[1,1,16,16]{3,2,1,0:T(8,128)} %param.11) | copy-start | bytes 3076

commit v3 on v2

--- a/solution.py
+++ b/solution.py
@@ -161,7 +161,9 @@
         for k in range(slots):
             buffer[receiver, LINES * k : LINES * k + LINES] = own_block(send_smem[receiver, k])[0:LINES]
 
-    gather_to(received, me)
+    gather_to(sent, me)
+    stay = pltpu.make_async_copy(sent.at[me], received.at[me], received_sem.at[me])
+    stay.start()
     pl.semaphore_wait(barrier, n_col + n_row - 2)
 
     def send_copy(peer):
@@ -225,6 +227,45 @@
         return carry
 
     lax.fori_loop(0, blocks // PREPARED, prepare, 0)
+
+    def partner_of(sender, k):
+        return jnp.maximum(partner_smem[sender, k], 0)
+
+    def compute_one(buffer, sender, group, slot, u):
+        k = group * GROUP + u
+        features = distance_features(tile_of(buffer[sender, LINES * k : LINES * k + LINES]))
+        squared = dot(coef[partner_of(sender, k)], features, (1, 0))
+        inverse = lax.rsqrt(squared)
+        cubed = inverse * inverse * inverse
+        high = cubed.astype(bf16)
+        highs[slot, u] = high
+        lows[slot, u] = (cubed - high.astype(f32)).astype(bf16)
+
+    def use_one(buffer, sender, group, slot, u):
+        k = group * GROUP + u
+        near_at = partner_of(sender, k)
+        block = buffer[sender, LINES * k : LINES * k + LINES]
+        high, low = highs[slot, u], lows[slot, u]
+        own_charge = charge[near_at]
+        sums = dot(own_charge, high, (1, 0))
+        sums = sums[0:16] + sums[16:32] + dot(own_charge[0:16], low, (1, 0))
+        valid = jnp.clip(partner_smem[sender, k] + 1, 0, 1).astype(f32)
+        rows = force_rows(block, sums) * valid
+        for l in range(3):
+            back[sender, l, k : k + 1] = rows[l : l + 1]
+        far_charge = charge_features(block)
+        sums = dot(far_charge, high, (1, 1))
+        sums = sums[0:16] + sums[16:32] + dot(far_charge[0:16], low, (1, 1))
+        rows = force_rows(own_block(near_at), sums)
+        for l in range(3):
+            near[l, sender, k : k + 1] = rows[l : l + 1]
+
+    def advance(later, now, slot):
+        for u in range(GROUP):
+            if later is not None:
+                compute_one(*later, 1 - slot, u)
+            if now is not None:
+                use_one(*now, slot, u)
 
     columns = lax.broadcasted_iota(i32, (blocks, 128), 1)
     moments = jnp.zeros((blocks, 128), f32)
@@ -251,49 +292,37 @@
 
     lax.fori_loop(1, n_col, moment_step, 0)
 
-    def partner_of(sender, k):
-        return jnp.maximum(partner_smem[sender, k], 0)
-
-    def compute(sender, group, slot):
-        for u in range(GROUP):
-            k = group * GROUP + u
-            features = distance_features(tile_of(received[sender, LINES * k : LINES * k + LINES]))
-            squared = dot(coef[partner_of(sender, k)], features, (1, 0))
-            inverse = lax.rsqrt(squared)
-            cubed = inverse * inverse * inverse
-            high = cubed.astype(bf16)
-            highs[slot, u] = high
-            lows[slot, u] = (cubed - high.astype(f32)).astype(bf16)
-
-    def use(sender, group, slot):
-        for u in range(GROUP):
-            k = group * GROUP + u
-            near_at = partner_of(sender, k)
-            block = received[sender, LINES * k : LINES * k + LINES]
-            high, low = highs[slot, u], lows[slot, u]
-            own_charge = charge[near_at]
-            sums = dot(own_charge, high, (1, 0))
-            sums = sums[0:16] + sums[16:32] + dot(own_charge[0:16], low, (1, 0))
-            valid = jnp.clip(partner_smem[sender, k] + 1, 0, 1).astype(f32)
-            rows = force_rows(block, sums) * valid
-            for l in range(3):
-                back[sender, l, k : k + 1] = rows[l : l + 1]
-            far_charge = charge_features(block)
-            sums = dot(far_charge, high, (1, 1))
-            sums = sums[0:16] + sums[16:32] + dot(far_charge[0:16], low, (1, 1))
-            rows = force_rows(own_block(near_at), sums)
-            for l in range(3):
-                near[l, sender, k : k + 1] = rows[l : l + 1]
-
     def sum_of(got, count):
         total = got[0]
         for at in range(1, count):
             total = total + got[at]
         return total
 
+    half = groups // 2
+    advance((sent, me, half), None, 1)
+    for group in range(half, groups - 1):
+        advance((sent, me, group + 1), (sent, me, group), (group - half) % 2)
+
     first = source(codes)
     arrival(first).wait_recv()
-    compute(first, 0, 0)
+    advance((received, first, 0), (sent, me, groups - 1), 1)
+
+    def sum_tops():
+        def wait_moments(step, carry):
+            peer = lax.rem(me + step, n_col)
+            cell_copy(peer, peer).wait_recv()
+            top_copy(peer, peer).wait_recv()
+            return carry
+
+        lax.fori_loop(1, n_col, wait_moments, 0)
+        row_sent[...] = sum_of(top_got, n_col)
+        row_got[my_row] = row_sent[...]
+
+        def row_step(step, carry):
+            row_copy(lax.rem(my_row + step, n_row), my_row).start()
+            return carry
+
+        lax.fori_loop(1, n_row, row_step, 0)
 
     def sender_step(step, carry):
         code, send_code = carry[0:2], carry[2:4]
@@ -305,45 +334,25 @@
         def _():
             send_step(step, send_code)
 
+        @pl.when(step == n_col // 2)
+        def _():
+            sum_tops()
+
         for group in range(groups - 1):
-            compute(sender, group + 1, (group + 1) % 2)
-            use(sender, group, group % 2)
-
-        @pl.when(step < n_col - 2)
-        def _():
-            arrival(following).wait_recv()
-
-        compute(following, 0, 0)
-        use(sender, groups - 1, (groups - 1) % 2)
-
-        @pl.when(step < n_col - 1)
-        def _():
-            back_copy(sender).start()
-
-        @pl.when(step == 4)
-        def _():
-            def wait_moments(other, inner):
-                peer = lax.rem(me + other, n_col)
-                cell_copy(peer, peer).wait_recv()
-                top_copy(peer, peer).wait_recv()
-                return inner
-
-            lax.fori_loop(1, n_col, wait_moments, 0)
-            cell_sum = sum_of(cell_got, n_col)
-            cell_rows = jnp.concatenate([cell_sum, jnp.zeros((128 - share, 128), f32)], axis=0)
-            cell_out[...] = jnp.transpose(cell_rows)[0:12, 0:share]
-            row_sent[...] = sum_of(top_got, n_col)
-            row_got[my_row] = row_sent[...]
-
-            def row_step(other, inner):
-                row_copy(lax.rem(my_row + other, n_row), my_row).start()
-                return inner
-
-            lax.fori_loop(1, n_row, row_step, 0)
-
+            advance((received, sender, group + 1), (received, sender, group), group % 2)
+        arrival(following).wait_recv()
+        advance((received, following, 0), (received, sender, groups - 1), (groups - 1) % 2)
+        back_copy(sender).start()
         return following_code + next_code(send_code)
 
-    lax.fori_loop(0, n_col, sender_step, codes + send_code)
+    lax.fori_loop(0, n_col - 1, sender_step, codes + send_code)
+
+    for group in range(half):
+        later = (received, me, group + 1) if group + 1 < half else None
+        advance(later, (received, me, group), group % 2)
+    cell_sum = sum_of(cell_got, n_col)
+    cell_rows = jnp.concatenate([cell_sum, jnp.zeros((128 - share, 128), f32)], axis=0)
+    cell_out[...] = jnp.transpose(cell_rows)[0:12, 0:share]
 
     returned[me] = back[me]
 
@@ -405,7 +414,7 @@
     cells = parent_cell.shape[1]
     share = cells // n_col
     vmem = pl.BlockSpec(memory_space=pltpu.VMEM)
-    hbm = pl.BlockSpec(memory_space=pl.ANY)
+    hbm = pl.BlockSpec(memory_space=pltpu.HBM)
     dma = pltpu.SemaphoreType.DMA
     force, cell, top = pl.pallas_call(
         functools.partial(kernel, n_row, n_col, slots),
@@ -452,7 +461,12 @@
             collective_id=0, has_side_effects=True, vmem_limit_bytes=40 * 1024 * 1024
         ),
         name="pair_forces",
-    )(positions[:, 0], strengths[:, 0], live_count, send_list[0, 0], partner[0, 0], parent_block, parent_cell)
+    )(*[
+        pltpu.with_memory_space_constraint(each, pltpu.HBM)
+        for each in (
+            positions[:, 0], strengths[:, 0], live_count, send_list[0, 0], partner[0, 0], parent_block, parent_cell
+        )
+    ])
     return force[:, None], cell[:, None, :], top
 
 

time: 66.5 us -> 59.3 us (0.89)
  local copies, waits for them, and re-layouts: 5.79 us -> 1.87 us
  Pallas kernels: 59.7 us -> 56.6 us
    unnamed x17 -> x3, local copies, waits for them, and re-layouts: 5.79 us -> 1.87 us
    pallas_call x1, Pallas kernels: 59.7 us -> 56.6 us  [body(): pl.pallas_call(functools.partial(kernel, n_row, n_col, slots), out_shape=...]
where the time goes in v3:
time: 59.3 us; the launch traced here: 59.1 us
  Pallas kernels  56.6 us (95%)
  local copies, waits for them, and re-layouts  1.87 us (3%)
  between operations  0.64 us (1%)
    pallas_call x1, Pallas kernels, body(): pl.pallas_call(functools.partial(kernel, n_row, n_col, slots), out_shape=...  56.6 us
    unnamed x3, local copies, waits for them, and re-layouts  1.87 us

profile of v3, /device:TPU:0, one launch (start us, length us, event | category | flops | bytes accessed | tf_op | source)
XLA Modules:
  0.0 59.1 jit_solution(15743176949107092149)
XLA Ops:
  0.6 56.6 %pair_forces.1 = (f32[3,64,256]{2,1,0:T(8,128)S(1)}, f32[12,16]{1,0:T(8,128)S(1)}, f32[12,64]{1,0:T(8,128)S(1)}) custom-call(f32[3,64,256]{2,1,0:T(8,128)} %bitcast.10, f32[3,64,256]{2,1,0:T(8,128)} %bitcast.11, s32[1,64]{1,0:T(1,128)} %live_in.1, s32[16,16]{1,0:T(8,128)} %bitcast.12, s32[16,16]{1,0:T(8,128)} %bitcast.13, s32[1,64]{1,0:T(1,128)} %parent_block_in.1, ...), custom_call_target="tpu_custom_call" | custom-call | tf_op jit(solution)/shard_map/pair_forces/pallas_call | solution.py:419
  57.3 0.6 %copy.11 = f32[12,1,16]{2,1,0:T(1,128)} copy(f32[12,1,16]{2,0,1:T(8,128)S(1)} %bitcast.9) | data formatting | bytes 1536
  57.9 0.7 %copy.14 = f32[3,1,64,256]{3,2,1,0:T(8,128)} copy(f32[3,1,64,256]{3,2,1,0:T(8,128)S(1)} %bitcast.8) | data formatting | bytes 393216
  58.5 0.6 %copy.15 = f32[12,64]{1,0:T(8,128)} copy(f32[12,64]{1,0:T(8,128)S(1)} %get-tuple-element.17) | data formatting | bytes 6144

commit v4 on v3

--- a/solution.py
+++ b/solution.py
@@ -96,7 +96,7 @@
     n_row, n_col, slots,
     pos_in, strength_in, live_in, send_in, partner_in, parent_block_in, parent_cell_in,
     force, cell_out, top_out,
-    pos, strength, live, send_smem, partner_smem, send_vmem, partner_vmem, parent_block, parent_cell, turned, own, coef, charge, sent, received, back, returned, near, highs, lows,
+    pos, strength, live, send_smem, partner_smem, send_vmem, partner_vmem, parent_block, parent_cell, turned, own, coef, charge, sent, received, back, returned, near, highs, lows, highs_turned, lows_turned,
     cell_sent, cell_got, top_sent, top_got, row_sent, row_got,
     sent_sem, received_sem, back_sem, returned_sem, cell_sent_sem, cell_got_sem, top_sent_sem, top_got_sem,
     row_sent_sem, row_got_sem, input_sem,
@@ -238,8 +238,11 @@
         inverse = lax.rsqrt(squared)
         cubed = inverse * inverse * inverse
         high = cubed.astype(bf16)
+        low = (cubed - high.astype(f32)).astype(bf16)
         highs[slot, u] = high
-        lows[slot, u] = (cubed - high.astype(f32)).astype(bf16)
+        lows[slot, u] = low
+        highs_turned[slot, u] = jnp.transpose(high)
+        lows_turned[slot, u] = jnp.transpose(low)
 
     def use_one(buffer, sender, group, slot, u):
         k = group * GROUP + u
@@ -254,8 +257,8 @@
         for l in range(3):
             back[sender, l, k : k + 1] = rows[l : l + 1]
         far_charge = charge_features(block)
-        sums = dot(far_charge, high, (1, 1))
-        sums = sums[0:16] + sums[16:32] + dot(far_charge[0:16], low, (1, 1))
+        sums = dot(far_charge, highs_turned[slot, u], (1, 0))
+        sums = sums[0:16] + sums[16:32] + dot(far_charge[0:16], lows_turned[slot, u], (1, 0))
         rows = force_rows(own_block(near_at), sums)
         for l in range(3):
             near[l, sender, k : k + 1] = rows[l : l + 1]
@@ -446,6 +449,8 @@
             pltpu.VMEM((3, n_col, slots, width), f32),
             pltpu.VMEM((2, GROUP, width, width), bf16),
             pltpu.VMEM((2, GROUP, width, width), bf16),
+            pltpu.VMEM((2, GROUP, width, width), bf16),
+            pltpu.VMEM((2, GROUP, width, width), bf16),
             pltpu.VMEM((n_col, share, 128), f32),
             pltpu.VMEM((n_col, share, 128), f32),
             pltpu.VMEM((16, 128), f32),

time: 59.3 us -> 52.2 us (0.88)
  Pallas kernels: 56.6 us -> 49.6 us
    pallas_call x1, Pallas kernels: 56.6 us -> 49.6 us  [body(): pl.pallas_call(functools.partial(kernel, n_row, n_col, slots), out_shape=...]
where the time goes in v4:
time: 52.2 us; the launch traced here: 52.1 us
  Pallas kernels  49.6 us (95%)
  local copies, waits for them, and re-layouts  1.87 us (4%)
  between operations  0.64 us (1%)
    pallas_call x1, Pallas kernels, body(): pl.pallas_call(functools.partial(kernel, n_row, n_col, slots), out_shape=...  49.6 us
    unnamed x3, local copies, waits for them, and re-layouts  1.87 us

profile of v4, /device:TPU:0, one launch (start us, length us, event | category | flops | bytes accessed | tf_op | source)
XLA Modules:
  0.0 52.1 jit_solution(15507102288914582071)
XLA Ops:
  0.6 49.6 %pair_forces.1 = (f32[3,64,256]{2,1,0:T(8,128)S(1)}, f32[12,16]{1,0:T(8,128)S(1)}, f32[12,64]{1,0:T(8,128)S(1)}) custom-call(f32[3,64,256]{2,1,0:T(8,128)} %bitcast.10, f32[3,64,256]{2,1,0:T(8,128)} %bitcast.11, s32[1,64]{1,0:T(1,128)} %live_in.1, s32[16,16]{1,0:T(8,128)} %bitcast.12, s32[16,16]{1,0:T(8,128)} %bitcast.13, s32[1,64]{1,0:T(1,128)} %parent_block_in.1, ...), custom_call_target="tpu_custom_call" | custom-call | tf_op jit(solution)/shard_map/pair_forces/pallas_call | solution.py:422
  50.2 0.6 %copy.11 = f32[12,1,16]{2,1,0:T(1,128)} copy(f32[12,1,16]{2,0,1:T(8,128)S(1)} %bitcast.9) | data formatting | bytes 1536
  50.8 0.7 %copy.14 = f32[3,1,64,256]{3,2,1,0:T(8,128)} copy(f32[3,1,64,256]{3,2,1,0:T(8,128)S(1)} %bitcast.8) | data formatting | bytes 393216
  51.5 0.6 %copy.15 = f32[12,64]{1,0:T(8,128)} copy(f32[12,64]{1,0:T(8,128)S(1)} %get-tuple-element.17) | data formatting | bytes 6144

commit v5 on v4

--- a/solution.py
+++ b/solution.py
@@ -10,7 +10,7 @@
 C2 = 64
 CORE_SQUARED = 1.0
 MOMENT_UNIT = 0.0625
-GROUP = 4
+GROUP = 8
 AHEAD = 6
 LINES = 6
 CHUNKS = 1
@@ -189,6 +189,12 @@
             src_ref=back.at[peer], dst_ref=returned.at[me], send_sem=back_sem.at[peer],
             recv_sem=returned_sem.at[me], device_id={"col": peer}, device_id_type=MESH)
 
+    def start_back(peer, group):
+        lines = slice(group * GROUP, group * GROUP + GROUP)
+        pltpu.make_async_remote_copy(
+            src_ref=back.at[peer, :, lines], dst_ref=returned.at[me, :, lines], send_sem=back_sem.at[peer],
+            recv_sem=returned_sem.at[me], device_id={"col": peer}, device_id_type=MESH).start()
+
     def back_arrival(peer):
         return pltpu.make_async_remote_copy(
             src_ref=back.at[peer], dst_ref=returned.at[peer], send_sem=back_sem.at[peer],
@@ -302,9 +308,10 @@
         return total
 
     half = groups // 2
-    advance((sent, me, half), None, 1)
+    base = groups - 1
+    advance((sent, me, half), None, (base - half) % 2)
     for group in range(half, groups - 1):
-        advance((sent, me, group + 1), (sent, me, group), (group - half) % 2)
+        advance((sent, me, group + 1), (sent, me, group), (base - group + 1) % 2)
 
     first = source(codes)
     arrival(first).wait_recv()
@@ -343,9 +350,10 @@
 
         for group in range(groups - 1):
             advance((received, sender, group + 1), (received, sender, group), group % 2)
+            start_back(sender, group)
         arrival(following).wait_recv()
         advance((received, following, 0), (received, sender, groups - 1), (groups - 1) % 2)
-        back_copy(sender).start()
+        start_back(sender, groups - 1)
         return following_code + next_code(send_code)
 
     lax.fori_loop(0, n_col - 1, sender_step, codes + send_code)

time: 52.2 us -> 52.1 us (level)
  no operation moved by 1% of the time
where the time goes in v5:
time: 52.1 us; the launch traced here: 51.9 us
  Pallas kernels  49.4 us (95%)
  local copies, waits for them, and re-layouts  1.87 us (4%)
  between operations  0.64 us (1%)
    pallas_call x1, Pallas kernels, body(): pl.pallas_call(functools.partial(kernel, n_row, n_col, slots), out_shape=...  49.4 us
    unnamed x3, local copies, waits for them, and re-layouts  1.87 us

profile of v5, /device:TPU:0, one launch (start us, length us, event | category | flops | bytes accessed | tf_op | source)
XLA Modules:
  0.0 51.9 jit_solution(5067290867495072818)
XLA Ops:
  0.6 49.4 %pair_forces.1 = (f32[3,64,256]{2,1,0:T(8,128)S(1)}, f32[12,16]{1,0:T(8,128)S(1)}, f32[12,64]{1,0:T(8,128)S(1)}) custom-call(f32[3,64,256]{2,1,0:T(8,128)} %bitcast.10, f32[3,64,256]{2,1,0:T(8,128)} %bitcast.11, s32[1,64]{1,0:T(1,128)} %live_in.1, s32[16,16]{1,0:T(8,128)} %bitcast.12, s32[16,16]{1,0:T(8,128)} %bitcast.13, s32[1,64]{1,0:T(1,128)} %parent_block_in.1, ...), custom_call_target="tpu_custom_call" | custom-call | tf_op jit(solution)/shard_map/pair_forces/pallas_call | solution.py:430
  50.1 0.6 %copy.11 = f32[12,1,16]{2,1,0:T(1,128)} copy(f32[12,1,16]{2,0,1:T(8,128)S(1)} %bitcast.9) | data formatting | bytes 1536
  50.7 0.7 %copy.14 = f32[3,1,64,256]{3,2,1,0:T(8,128)} copy(f32[3,1,64,256]{3,2,1,0:T(8,128)S(1)} %bitcast.8) | data formatting | bytes 393216
  51.3 0.6 %copy.15 = f32[12,64]{1,0:T(8,128)} copy(f32[12,64]{1,0:T(8,128)S(1)} %get-tuple-element.17) | data formatting | bytes 6144
